TPU v7x, 512 devices: a whole 4x8x8 slice. The times are simulated.
512 devices in a mesh: rep: 4 (over x), expert: 128 (over z, y, core).
Axes of the slice: x: 4, y: 8, z: 8, core: 2. Of those that a mesh axis runs over, the one named last changes fastest.
Arguments:
- tokens: bfloat16 [65536, 1536], P(('rep', 'expert')), may hold values from -6 to 6
- routes: int32 [65536, 4], P(('rep', 'expert')), may hold values from 0 to 127, all different within a row; in each aligned block of 128 rows (0 to 127, 128 to 255, ...) at most 5 rows name the same one
- gates: bfloat16 [65536, 4], P(('rep', 'expert')), may hold values from 0.049804688 to 1
- output_grad: bfloat16 [65536, 1536], P(('rep', 'expert')), may hold values from -6 to 6
- w_in: bfloat16 [128, 1536, 768], P('expert', 'rep'), may hold values from -0.15625 to 0.15625
- w_out: bfloat16 [128, 384, 1536], P('expert', None, 'rep'), may hold values from -0.3125 to 0.3125
- momentum_in: bfloat16 [128, 1536, 768], P('expert', 'rep'), may hold values from -24 to 24
- momentum_out: bfloat16 [128, 384, 1536], P('expert', None, 'rep'), may hold values from -24 to 24
Outputs:
- token_grad: bfloat16 [65536, 1536], P(('rep', 'expert'))
- gate_grad: bfloat16 [65536, 4], P(('rep', 'expert'))
- new_momentum_in: bfloat16 [128, 1536, 768], P('expert', 'rep')
- new_momentum_out: bfloat16 [128, 384, 1536], P('expert', None, 'rep')
Inputs may be any that keep to these rules, and one draw needn't show every extreme that they name: `routes`: each row names 4 different experts. Within the 128 rows of one device no expert is named by more than 5 rows, and on some devices one expert is named by exactly 5 rows.
All inputs are finite; a program needn't handle non-finite values.
Results may differ from a plain program's by a relative error of at most 0.012.
Values may be sent and summed in bfloat16 or wider, within the bound.
A program may use at most 64 MiB of HBM per device.

v0:
```python
import math

import jax
import jax.numpy as jnp
from jax import lax
from jax.sharding import PartitionSpec as P

momentum_decay = 0.9


def in_one_piece(arrays, axis, split_dim, concat_dim, along):
    widths = [math.prod(a.shape[along:]) for a in arrays]
    both = jnp.concatenate(
        [a.reshape(*a.shape[:along], w) for a, w in zip(arrays, widths)], axis=along
    )
    out = lax.all_to_all(both, axis, split_axis=split_dim, concat_axis=concat_dim, tiled=True)
    blocks = jnp.split(out, [sum(widths[:k]) for k in range(1, len(widths))], axis=along)
    return tuple((b.reshape(*out.shape[:along], *a.shape[along:]) for a, b in zip(arrays, blocks)))


def slot_positions(routes, experts):
    flat_routes = routes.reshape(-1)
    one_hot = (flat_routes[:, None] == jnp.arange(experts, dtype=jnp.int32)[None, :]).astype(
        jnp.int32
    )
    earlier = jnp.cumsum(one_hot, axis=0) - one_hot
    return jnp.sum(earlier * one_hot, axis=1)


def forward_pass(x_rows, weight_in, weight_out):
    width_ffn = weight_out.shape[0]
    both = jnp.dot(x_rows, weight_in, preferred_element_type=jnp.float32)
    gate_pre = both[:, :width_ffn]
    up_part = both[:, width_ffn:]
    silu_gate = jax.nn.silu(gate_pre)
    hidden = (silu_gate * up_part).astype(jnp.bfloat16)
    expert_out = jnp.dot(hidden, weight_out, preferred_element_type=jnp.float32)
    return (gate_pre, up_part, silu_gate, hidden, expert_out)


def per_device(tokens, routes, gates, output_grad, w_in, w_out, momentum_in, momentum_out):
    tok_dev, width = tokens.shape
    top_count = routes.shape[1]
    senders = lax.axis_size("expert")
    local_count = w_in.shape[0]
    experts = senders * local_count
    capacity = max(2, min(tok_dev, 5 * tok_dev * top_count // (4 * experts)))
    slot_count = experts * capacity
    target = routes.reshape(-1) * capacity + slot_positions(routes, experts)
    token_ids = jnp.repeat(jnp.arange(tok_dev, dtype=jnp.int32), top_count)
    source_row = jnp.full((slot_count,), tok_dev, jnp.int32).at[target].set(token_ids)
    slot_gate = jnp.zeros((slot_count,), jnp.bfloat16).at[target].set(gates.reshape(-1))
    zero_row = jnp.zeros((1, width), jnp.bfloat16)
    sent_tokens = jnp.concatenate([tokens, zero_row], axis=0)[source_row].reshape(
        experts, capacity, width
    )
    sent_grads = jnp.concatenate([output_grad, zero_row], axis=0)[source_row].reshape(
        experts, capacity, width
    )
    sent_gate = slot_gate.reshape(experts, capacity)
    whole_in, whole_out = (
        lax.all_gather(w_in, "rep", axis=1, tiled=True),
        lax.all_gather(w_out, "rep", axis=2, tiled=True),
    )

    def local_rows(received, expert):
        shaped = received.reshape((senders, local_count) + received.shape[1:])
        return shaped[:, expert].reshape((senders * capacity,) + received.shape[2:])

    got_tokens, got_gate = in_one_piece((sent_tokens, sent_gate), "expert", 0, 0, 2)
    forward = [forward_pass(local_rows(got_tokens, 0), whole_in[0], whole_out[0])]
    got_grads = lax.all_to_all(sent_grads, "expert", split_axis=0, concat_axis=0, tiled=True)
    expert = 0
    gate_pre, up_part, silu_gate, hidden, expert_out = forward[expert]
    dy_rows = local_rows(got_grads, expert)
    gate_grad = jnp.sum(expert_out * dy_rows.astype(jnp.float32), axis=1).astype(jnp.bfloat16)
    scaled = (
        local_rows(got_gate, expert).astype(jnp.float32)[:, None] * dy_rows.astype(jnp.float32)
    ).astype(jnp.bfloat16)
    scaled_rows = [scaled]
    gate_rows = [gate_grad]
    parts_out = [
        lax.dot_general(
            hidden, scaled, (((0,), (0,)), ((), ())), preferred_element_type=jnp.float32
        )
    ]
    grad_out_all = jnp.stack(parts_out)
    expert = 0
    gate_pre, up_part, silu_gate, hidden, expert_out = forward[expert]
    hidden_grad = lax.dot_general(
        scaled_rows[expert],
        whole_out[expert],
        (((1,), (1,)), ((), ())),
        preferred_element_type=jnp.float32,
    )
    sigma = jax.nn.sigmoid(gate_pre)
    dgu = jnp.concatenate(
        [hidden_grad * up_part * sigma * (1.0 + gate_pre * (1.0 - sigma)), hidden_grad * silu_gate],
        axis=1,
    ).astype(jnp.bfloat16)
    row_grad = lax.dot_general(
        dgu, whole_in[expert], (((1,), (1,)), ((), ())), preferred_element_type=jnp.float32
    ).astype(jnp.bfloat16)
    row_grads = row_grad.reshape(senders, 1, capacity, width)
    parts_in = [
        lax.dot_general(
            local_rows(got_tokens, expert),
            dgu,
            (((0,), (0,)), ((), ())),
            preferred_element_type=jnp.float32,
        )
    ]
    grad_in_all = jnp.stack(parts_in)
    back_send = row_grads.reshape(experts, capacity, width)
    gate_send = jnp.stack([item.reshape(senders, capacity) for item in gate_rows], axis=1).reshape(
        experts, capacity
    )
    back_rows, back_gate = (
        lax.all_to_all(back_send, "expert", split_axis=0, concat_axis=0, tiled=True),
        lax.all_to_all(gate_send, "expert", split_axis=0, concat_axis=0, tiled=True),
    )
    picked = back_rows.reshape(slot_count, width)[target].reshape(tok_dev, top_count, width)
    token_grad = jnp.sum(picked.astype(jnp.float32), axis=1).astype(jnp.bfloat16)
    gate_grad_out = back_gate.reshape(-1)[target].reshape(tok_dev, top_count)
    summed_in, summed_out = (
        lax.psum_scatter(
            grad_in_all.astype(jnp.bfloat16), "rep", scatter_dimension=1, tiled=True
        ).astype(jnp.float32),
        lax.psum_scatter(
            grad_out_all.astype(jnp.bfloat16), "rep", scatter_dimension=2, tiled=True
        ).astype(jnp.float32),
    )
    new_momentum_in = (momentum_decay * momentum_in.astype(jnp.float32) + summed_in).astype(
        jnp.bfloat16
    )
    new_momentum_out = (momentum_decay * momentum_out.astype(jnp.float32) + summed_out).astype(
        jnp.bfloat16
    )
    return (token_grad, gate_grad_out, new_momentum_in, new_momentum_out)


def solution(mesh):
    in_specs = (
        P(("rep", "expert"), None),
        P(("rep", "expert"), None),
        P(("rep", "expert"), None),
        P(("rep", "expert"), None),
        P("expert", "rep", None),
        P("expert", None, "rep"),
        P("expert", "rep", None),
        P("expert", None, "rep"),
    )
    out_specs = (
        P(("rep", "expert"), None),
        P(("rep", "expert"), None),
        P("expert", "rep", None),
        P("expert", None, "rep"),
    )
    return jax.shard_map(
        per_device, mesh=mesh, in_specs=in_specs, out_specs=out_specs, check_vma=False
    )
```

profile of v0, /device:TPU:1, one launch (start us, length us, event | category | flops | bytes accessed | tf_op | source)
XLA Modules:
  0.0 363.6 jit_solution(14490105411848876675)
XLA Ops:
  7.2 0.7 broadcast_multiply_fusion
  7.9 0.8 copy.27
  8.7 0.1 eq.29
  8.8 0.1 eq.25
  8.9 0.1 copy.26
  9.0 0.1 mul.71
  9.1 0.1 copy.29
  9.4 0.2 fusion.12
  9.7 0.2 fusion.11
  9.9 2.4 scatter_custom_fusion
  12.5 3.1 gather_fusion.1
  15.6 2.5 reshape.117
  18.0 19.0 %all-to-all-start.1 = ((bf16[128,5,1536]{2,1,0:T(8,128)(2,1)}), bf16[128,5,1536]{2,1,0:T(8,128)(2,1)}, u32[]{:S(2)}, u32[]{:S(2)}) async-start(bf16[128,5,1536]{2,1,0:T(8,128)(2,1)} %reshape.117), calls=%async_computation.1 | async-start | bytes 6291456 | tf_op jit(solution)/shard_map/all_to_all | solution.py:72
  37.0 0.1 copy.31
  37.1 0.1 reshape.169
  37.3 3.8 %scatter_custom_fusion.1 = bf16[640]{0:T(1024)(128)(2,1)S(1)} fusion(s32[512]{0:T(512)S(1)} %bitcast.54, bf16[512]{0:T(512)(128)(2,1)S(1)} %reshape.169, bf16[]{:T(256)} %constant.9.clone.1), kind=kCustom, calls=%fused_computation.50 | custom fusion | bytes 1282 | tf_op jit(solution)/shard_map/scatter | solution.py:52
  41.0 0.3 reshape_reshape.8
  41.3 3.7 %gather_fusion = bf16[640,1536]{1,0:T(8,128)(2,1)} fusion(bf16[129,1536]{1,0:T(8,128)(2,1)S(1)} %concatenate.13, s32[1024]{0:T(1024)S(1)} %pad_clamp_fusion.1), kind=kCustom, calls=%fused_computation | custom fusion | bytes 3934720 | tf_op jit(solution)/shard_map/gather | solution.py:54
  45.0 2.7 reshape.115
  47.7 2.4 pad_maximum_fusion
  50.1 59.3 %all-to-all-done.1 = bf16[128,5,1536]{2,1,0:T(8,128)(2,1)} async-done(((bf16[128,5,1536]{2,1,0:T(8,128)(2,1)}), bf16[128,5,1536]{2,1,0:T(8,128)(2,1)}, u32[]{:S(2)}, u32[]{:S(2)}) %all-to-all-start.1) | async-done | bytes 1966112 | tf_op jit(solution)/shard_map/all_to_all | solution.py:72
  109.4 11.7 %all-to-all-start = ((bf16[128,5,1537]{2,1,0:T(8,128)(2,1)}), bf16[128,5,1537]{2,1,0:T(8,128)(2,1)S(1)}, u32[]{:S(2)}, u32[]{:S(2)}) async-start(bf16[128,5,1537]{2,1,0:T(8,128)(2,1)} %pad_maximum_fusion), calls=%async_computation | async-start | bytes 6815744 | tf_op jit(solution)/shard_map/all_to_all | solution.py:16
  121.2 0.7 all-gather.5.cloned.1.call-update
  121.9 0.7 all-gather.3.cloned.1.call-update
  122.7 4.6 %reshape.123 = f32[640,1536]{1,0:T(8,128)} reshape(bf16[128,5,1536]{2,1,0:T(8,128)(2,1)} %all-to-all-done.1) | data formatting | bytes 5898240 | tf_op jit(solution)/shard_map/convert_element_type | solution.py:78
  127.3 72.4 %all-to-all-done = bf16[128,5,1537]{2,1,0:T(8,128)(2,1)S(1)} async-done(((bf16[128,5,1537]{2,1,0:T(8,128)(2,1)}), bf16[128,5,1537]{2,1,0:T(8,128)(2,1)S(1)}, u32[]{:S(2)}, u32[]{:S(2)}) %all-to-all-start) | async-done | bytes 1967392 | tf_op jit(solution)/shard_map/all_to_all | solution.py:16
  199.6 0.2 fusion.15
  199.9 0.2 reshape.124
  200.1 0.8 slice_convert_fusion
  200.9 1.9 copy.40
  202.8 1.9 split.9
  204.7 4.3 %reshape_squeeze_reshape.2 = bf16[640,1536]{1,0:T(8,128)(2,1)} reshape(bf16[128,5,1536]{2,1,0:T(8,128)(2,1)} %split.9) | data formatting | bytes 3932160 | tf_op jit(solution)/shard_map/reshape;squeeze;reshape | solution.py:68
  209.0 2.5 multiply_convert_fusion
  211.5 2.2 convert_element_type.100
  213.7 5.8 %fusion.3 = f32[640,768]{0,1:T(8,128)} fusion(bf16[640,1536]{1,0:T(8,128)(2,1)} %reshape_squeeze_reshape.2, bf16[1,1536,768]{2,1,0:T(8,128)(2,1)} %all-gather.5.cloned.1.call-done), kind=kOutput, calls=%fused_computation.16 | convolution fusion | flops 1509949440 | bytes 6291456 | tf_op jit(solution)/shard_map/dot_general | solution.py:32
  219.5 4.2 %multiply_convert_fusion.5 = (bf16[640,384]{0,1:T(8,128)(2,1)}, bf16[640,384]{0,1:T(8,128)(2,1)}, bf16[640,384]{0,1:T(8,128)(2,1)S(1)}) fusion(f32[640,768]{0,1:T(8,128)} %fusion.3, bf16[640,1536]{1,0:T(8,128)(2,1)S(1)} %copy-done.1, bf16[1,384,1536]{2,1,0:T(8,128)(2,1)} %all-gather.3.cloned.1.call-done), kind=kOutput, calls=%fused_computation.27 | convolution fusion | flops 758661120 | bytes 6586368 | tf_op jit(solution)/shard_map/dot_general | solution.py:90
  223.7 0.8 copy-done.2
  224.5 1.2 fusion.1
  225.7 3.3 copy.41
  229.0 1.3 copy.45
  230.4 5.0 %fusion = bf16[1,1536,768]{2,1,0:T(8,128)(2,1)} fusion(bf16[640,1536]{1,0:T(8,128)(2,1)} %reshape_squeeze_reshape.2, bf16[640,384]{0,1:T(8,128)(2,1)S(1)} %copy-done.11, bf16[640,384]{0,1:T(8,128)(2,1)S(1)} %copy-done.10), kind=kOutput, calls=%fused_computation.12 | convolution fusion | flops 1513095168 | bytes 5308416 | tf_op jit(solution)/shard_map/dot_general | solution.py:106
  235.5 1.0 copy-done.3
  236.5 0.4 copy-done.4
  236.9 3.4 multiply_reduce_fusion
  240.3 0.9 convert_element_type.123
  241.2 12.9 %all-to-all-start.3 = ((bf16[128,1,5]{2,1,0:T(2,128)(2,1)}), bf16[128,1,5]{2,1,0:T(2,128)(2,1)S(1)}, u32[]{:S(2)}, u32[]{:S(2)}) async-start(bf16[128,1,5]{2,1,0:T(2,128)(2,1)} %convert_element_type.123), calls=%async_computation.3 | async-start | bytes 131072 | tf_op jit(solution)/shard_map/all_to_all | solution.py:120
  254.1 3.4 convolution_convert_fusion.1
  257.5 2.5 reshape_reshape.7
  260.0 5.5 %all-to-all-done.3 = bf16[128,1,5]{2,1,0:T(2,128)(2,1)S(1)} async-done(((bf16[128,1,5]{2,1,0:T(2,128)(2,1)}), bf16[128,1,5]{2,1,0:T(2,128)(2,1)S(1)}, u32[]{:S(2)}, u32[]{:S(2)}) %all-to-all-start.3) | async-done | bytes 1312 | tf_op jit(solution)/shard_map/all_to_all | solution.py:120
  265.5 8.7 %all-to-all-start.2 = ((bf16[128,5,1536]{2,1,0:T(8,128)(2,1)}), bf16[128,5,1536]{2,1,0:T(8,128)(2,1)}, u32[]{:S(2)}, u32[]{:S(2)}) async-start(bf16[128,5,1536]{2,1,0:T(8,128)(2,1)} %reshape_reshape.7), calls=%async_computation.2 | async-start | bytes 6291456 | tf_op jit(solution)/shard_map/all_to_all | solution.py:119
  274.2 0.2 reduce.1
  274.4 0.2 reshape.120
  274.6 3.5 gather_fusion.3
  278.1 0.1 reshape.121
  278.2 0.7 copy.38
  278.9 1.3 reshape_bitcast_fusion
  280.1 0.9 copy.42
  281.0 0.8 add_convert_fusion.1
  281.8 64.7 %all-to-all-done.2 = bf16[128,5,1536]{2,1,0:T(8,128)(2,1)} async-done(((bf16[128,5,1536]{2,1,0:T(8,128)(2,1)}), bf16[128,5,1536]{2,1,0:T(8,128)(2,1)}, u32[]{:S(2)}, u32[]{:S(2)}) %all-to-all-start.2) | async-done | bytes 1966112 | tf_op jit(solution)/shard_map/all_to_all | solution.py:119
  346.6 3.0 reshape.118
  349.6 2.1 gather_fusion.2
  351.7 0.4 reshape.119
  352.1 2.8 reduce_sum.34
  355.0 2.1 add_convert_fusion
  (45 shorter events, 0.5 us)
Async XLA Ops:
  7.2 5.3 %copy-start.6 = (bf16[128,1536]{1,0:T(8,128)(2,1)S(1)}, bf16[128,1536]{1,0:T(8,128)(2,1)}, u32[]{:S(2)}) copy-start(bf16[128,1536]{1,0:T(8,128)(2,1)} %param.11) | copy-start | bytes 1179652
  18.0 19.0 %copy-start.9 = (bf16[128,4]{0,1:T(4,128)(2,1)S(1)}, bf16[128,4]{0,1:T(4,128)(2,1)}, u32[]{:S(2)}) copy-start(bf16[128,4]{0,1:T(4,128)(2,1)} %param.10) | copy-start | bytes 3076
  18.0 23.3 %copy-start.7 = (bf16[128,1536]{1,0:T(8,128)(2,1)S(1)}, bf16[128,1536]{1,0:T(8,128)(2,1)}, u32[]{:S(2)}) copy-start(bf16[128,1536]{1,0:T(8,128)(2,1)} %param.8) | copy-start | bytes 1179652
  18.0 91.4 %all-to-all-start.1 = ((bf16[128,5,1536]{2,1,0:T(8,128)(2,1)}), bf16[128,5,1536]{2,1,0:T(8,128)(2,1)}, u32[]{:S(2)}, u32[]{:S(2)}) async-start(bf16[128,5,1536]{2,1,0:T(8,128)(2,1)} %reshape.117), calls=%async_computation.1 | async-start | bytes 6291456 | tf_op jit(solution)/shard_map/all_to_all | solution.py:72
  109.4 90.2 %all-to-all-start = ((bf16[128,5,1537]{2,1,0:T(8,128)(2,1)}), bf16[128,5,1537]{2,1,0:T(8,128)(2,1)S(1)}, u32[]{:S(2)}, u32[]{:S(2)}) async-start(bf16[128,5,1537]{2,1,0:T(8,128)(2,1)} %pad_maximum_fusion), calls=%async_computation | async-start | bytes 6815744 | tf_op jit(solution)/shard_map/all_to_all | solution.py:16
  121.1 92.6 %all-gather.5.cloned.1.call-start = ((), (), s32[]{:S(2)}) async-start(), calls=%async_computation.7 | async-start | bytes 2949120 | tf_op jit(solution)/shard_map/all_gather | solution.py:62
  121.9 97.6 %all-gather.3.cloned.1.call-start = ((), (), s32[]{:S(2)}) async-start(), calls=%async_computation.6 | async-start | bytes 1474560 | tf_op jit(solution)/shard_map/all_gather | solution.py:63
  122.6 156.2 %reduce-scatter.7.cloned.1.call-start = ((), (), s32[]{:S(2)}) async-start(), calls=%async_computation.9 | async-start | bytes 1474560
  213.7 5.8 %copy-start.1 = (bf16[640,1536]{1,0:T(8,128)(2,1)S(1)}, bf16[640,1536]{1,0:T(8,128)(2,1)}, u32[]{:S(2)}) copy-start(bf16[640,1536]{1,0:T(8,128)(2,1)} %convert_element_type.100) | copy-start | bytes 5898244
  219.5 5.0 %copy-start = (f32[640,1536]{1,0:T(8,128)S(1)}, f32[640,1536]{1,0:T(8,128)}, u32[]{:S(2)}) copy-start(f32[640,1536]{1,0:T(8,128)} %reshape.123) | copy-start | bytes 11796484
  223.7 0.8 copy-start.2
  229.0 1.4 copy-start.10
  229.0 1.4 copy-start.11
  230.3 124.6 %reduce-scatter.5.cloned.1.call-start = ((), (), s32[]{:S(2)}) async-start(), calls=%async_computation.8 | async-start | bytes 2949120 | tf_op jit(solution)/shard_map/reduce_scatter | solution.py:126
  235.4 1.0 copy-start.3
  235.4 1.4 copy-start.4
  241.2 24.3 %all-to-all-start.3 = ((bf16[128,1,5]{2,1,0:T(2,128)(2,1)}), bf16[128,1,5]{2,1,0:T(2,128)(2,1)S(1)}, u32[]{:S(2)}, u32[]{:S(2)}) async-start(bf16[128,1,5]{2,1,0:T(2,128)(2,1)} %convert_element_type.123), calls=%async_computation.3 | async-start | bytes 131072 | tf_op jit(solution)/shard_map/all_to_all | solution.py:120
  265.5 81.1 %all-to-all-start.2 = ((bf16[128,5,1536]{2,1,0:T(8,128)(2,1)}), bf16[128,5,1536]{2,1,0:T(8,128)(2,1)}, u32[]{:S(2)}, u32[]{:S(2)}) async-start(bf16[128,5,1536]{2,1,0:T(8,128)(2,1)} %reshape_reshape.7), calls=%async_computation.2 | async-start | bytes 6291456 | tf_op jit(solution)/shard_map/all_to_all | solution.py:119
  274.1 6.9 %copy-start.8 = (bf16[1,384,384]{2,1,0:T(8,128)(2,1)S(1)}, bf16[1,384,384]{2,1,0:T(8,128)(2,1)}, u32[]{:S(2)}) copy-start(bf16[1,384,384]{2,1,0:T(8,128)(2,1)} %param.15) | copy-start | bytes 884740
  352.1 2.9 copy-start.5
Sparse Core Ops, SparseCore 0:
  124.1 39.1 all-gather.4
  165.4 29.2 all-gather.2
  230.5 28.2 reduce-scatter.6
  261.4 38.0 reduce-scatter.4
where the time goes:
time: 367 us; the launch traced here: 364 us
  waiting for transfers between devices  203 us (55%)
  local copies, waits for them, and re-layouts  57.7 us (16%)
  starting transfers between devices  52.4 us (14%)
  matrix products  23 us (6%)
  between operations  14.1 us (4%)
  other arithmetic  13.1 us (4%)
    all_to_all x1, waiting for transfers between devices, in_one_piece(): lax.all_to_all(both, axis, split_axis=split_dim, concat_axis=concat_dim,...  72.4 us
    all_to_all x1, waiting for transfers between devices, per_device(): lax.all_to_all(back_send, 'expert', split_axis=0, concat_axis=0, tiled=True)  64.7 us
    all_to_all x1, waiting for transfers between devices, per_device(): lax.all_to_all(sent_grads, 'expert', split_axis=0, concat_axis=0, tiled=T...  59.3 us
    all_to_all x1, starting transfers between devices, per_device(): lax.all_to_all(sent_grads, 'expert', split_axis=0, concat_axis=0, tiled=T...  19 us
    all_to_all x1, starting transfers between devices, per_device(): lax.all_to_all(gate_send, 'expert', split_axis=0, concat_axis=0, tiled=True)  12.9 us
    all_to_all x1, starting transfers between devices, in_one_piece(): lax.all_to_all(both, axis, split_axis=split_dim, concat_axis=concat_dim,...  11.7 us
    unnamed x32, local copies, waits for them, and re-layouts  10.5 us
    all_to_all x1, starting transfers between devices, per_device(): lax.all_to_all(back_send, 'expert', split_axis=0, concat_axis=0, tiled=True)  8.68 us
  transfers between devices with their start and end apart: 8, of which 4 were waited for; matrix products, arithmetic and copies ran while one was open for 19% of the time, Pallas kernels for 0%

commit v1 on v0

v1 whole, which is shorter than its diff:
```python
import functools

import jax
import jax.numpy as jnp
from jax import lax
from jax.experimental import pallas as pl
from jax.experimental.pallas import tpu as pltpu
from jax.sharding import PartitionSpec as P


decay = 0.9
f32, bf16, i32 = jnp.float32, jnp.bfloat16, jnp.int32
PEERS, TOK, WIDTH, HALF, FFN, CAP, TOP, REPS = 128, 128, 1536, 768, 384, 5, 4, 4
ROWS = PEERS * CAP
UNIT = 16 * CAP
by_mesh = pl.DeviceIdType.MESH


def iota(shape, dim):
    return lax.broadcasted_iota(i32, shape, dim)


def dot(a, b, over=(1, 0)):
    return lax.dot_general(a, b, (((over[0],), (over[1],)), ((), ())), preferred_element_type=f32)


def kernel(
    tok_ref, routes_ref, gates_ref, dy_ref, w_in_ref, w_out_ref, mom_in_ref, mom_out_ref,
    token_grad_ref, gate_grad_ref, new_in_ref, new_out_ref,
    pick, pack, gate_rows, send, recv, back_send, back_recv,
    x_rows, scaled, dy_half, scale_col, win, wout, gate_up, hidden, dh, dgu, row_grad, gg,
    part_in, part_out, got_in, got_out,
    send_sem, recv_sem, back_send_sem, back_recv_sem, w_send, w_recv, in_send, in_recv, out_send, out_recv,
):
    rep = lax.axis_index("rep")
    me = lax.axis_index("expert")
    z, y, core = me // 16, (me // 2) % 8, me % 2

    def peer(j, sign):
        m = j // 2
        dz, dy, dc = m % 8, (m // 8 + m) % 8, j % 2
        return ((z + sign * dz + 8) % 8) * 16 + ((y + sign * dy + 8) % 8) * 2 + (core + dc) % 2

    barrier = pltpu.get_barrier_semaphore()

    @pl.loop(1, PEERS)
    def _(j):
        pl.semaphore_signal(barrier, inc=1, device_id=(rep, peer(j, 1)), device_id_type=by_mesh)

    for d in range(1, REPS):
        pl.semaphore_signal(barrier, inc=1, device_id=((rep + d) % REPS, me), device_id_type=by_mesh)

    expert_of = iota((PEERS, TOK), 0)
    before = (iota((TOK, TOK), 0) < iota((TOK, TOK), 1)).astype(f32).astype(bf16)
    base = jnp.zeros((PEERS, 1), f32)
    keys = []
    routes = routes_ref[...]
    gates = gates_ref[...].astype(f32)
    for k in range(TOP):
        route = routes[k : k + 1, :]
        named = (expert_of == route).astype(f32)
        count = dot(named.astype(bf16), before) + base
        slot = jnp.sum(named * count, axis=0, keepdims=True)
        base = base + jnp.sum(named, axis=1, keepdims=True)
        keys.append(route * 8 + slot.astype(i32))

    def key_of(j):
        m = j >> 1
        ez = (z + (m & 7)) & 7
        ey = (y + (((m >> 3) + m) & 7)) & 7
        return (ez * 16 + ey * 2 + ((core + (j & 1)) & 1)) * 8

    @pl.loop(0, 8)
    def _(q):
        r = iota((256, TOK), 0) & 15
        i = (r * 13) >> 6
        key = key_of(q * 16 + (iota((256, TOK), 0) >> 4)) + (r - i * 5)
        hit = functools.reduce(jnp.logical_or, [key == k for k in keys])
        for n in range(3):
            here = jnp.logical_and(hit, i == n)
            pick[pl.ds(q * 256, 256), n * 128 : (n + 1) * 128] = jnp.where(here, 1.0, 0.0).astype(bf16)

    own_key = key_of(iota((PEERS, TOK), 0))
    lane = iota((PEERS, 128), 1)
    rows = jnp.zeros((PEERS, 128), f32)
    for s in range(CAP):
        val = sum(jnp.where(own_key + s == keys[k], gates[k : k + 1, :], 0.0) for k in range(TOP))
        rows = rows + jnp.where(lane == s, jnp.sum(val, axis=1, keepdims=True), 0.0)
    gate_rows[...] = rows

    a, col = iota((4 * UNIT, 256), 0), iota((4 * UNIT, 256), 1)
    kind = (a >= UNIT).astype(i32) + (a >= 2 * UNIT).astype(i32) + (a >= 3 * UNIT).astype(i32)
    rr = a - kind * UNIT
    c16 = (rr * 205) >> 10
    want = c16 * 16 + jnp.where(kind == 3, 15, kind * 5 + rr - c16 * 5)
    pack[...] = (col == want).astype(f32).astype(bf16)

    u_iota = iota((UNIT, 128), 0)
    slot_lane = iota((UNIT, 128), 1) == u_iota - ((u_iota * 205) >> 10) * 5

    def gather(p):
        src, h = (tok_ref, p) if p < 2 else (dy_ref, p - 2)
        first = h * HALF
        blocks = [src[:, first + b * 128 : first + (b + 1) * 128] for b in range(6)]
        table = jnp.concatenate(
            [jnp.concatenate(blocks[0:3], axis=0), jnp.concatenate(blocks[3:6], axis=0)], axis=1
        )

        @pl.loop(0, 8)
        def _(q):
            out = dot(pick[pl.ds(q * 256, 256), :], table)
            left = out[:, :128].reshape(16, 16, 128)
            if p == 0:
                own = gate_rows[pl.ds(q * 16, 16), :].reshape(16, 1, 128)
                left = left + jnp.where(iota((16, 16, 128), 1) == 15, own, 0.0)
            send[p, pl.ds(q * 16, 16), 0:16, :] = left.astype(bf16)
            send[p, pl.ds(q * 16, 16), 16:32, :] = out[:, 128:].reshape(16, 16, 128).astype(bf16)

    def send_pass(p):
        pltpu.make_async_copy(send.at[p, 0], recv.at[p, 0], recv_sem.at[p]).start()

        @pl.loop(1, PEERS)
        def _(j):
            pltpu.make_async_remote_copy(
                send.at[p, j], recv.at[p, j], send_sem.at[p], recv_sem.at[p],
                device_id=(rep, peer(j, 1)), device_id_type=by_mesh,
            ).start()

    def send_back(h):
        pltpu.make_async_copy(back_send.at[h, 0], back_recv.at[h, 0], back_recv_sem.at[h]).start()

        @pl.loop(1, PEERS)
        def _(j):
            pltpu.make_async_remote_copy(
                back_send.at[h, j], back_recv.at[h, j], back_send_sem.at[h], back_recv_sem.at[h],
                device_id=(rep, peer(j, -1)), device_id_type=by_mesh,
            ).start()

    def wait_all(ref, sem):
        pltpu.make_async_copy(ref, ref, sem).wait()

    gather(0)
    pl.semaphore_wait(barrier, PEERS - 1 + REPS - 1)
    send_pass(0)

    mine = pl.ds(pl.multiple_of(rep * FFN, FFN), FFN)
    own_in = pltpu.make_async_copy(w_in_ref, win.at[mine], w_recv.at[0])
    own_out = pltpu.make_async_copy(w_out_ref, wout.at[rep], w_recv.at[1])
    own_in.start()
    own_out.start()
    for d in range(1, REPS):
        pltpu.make_async_remote_copy(
            w_in_ref, win.at[mine], w_send.at[0], w_recv.at[0],
            device_id=((rep + d) % REPS, me), device_id_type=by_mesh,
        ).start()
    for d in range(1, REPS):
        pltpu.make_async_remote_copy(
            w_out_ref, wout.at[rep], w_send.at[1], w_recv.at[1],
            device_id=((rep + d) % REPS, me), device_id_type=by_mesh,
        ).start()
    for p in range(1, 4):
        gather(p)
        send_pass(p)

    def unpack(p):
        wait_all(recv.at[p], recv_sem.at[p])
        first = (p % 2) * HALF

        @pl.loop(0, 8)
        def _(u):
            left = recv[p, pl.ds(u * 16, 16), 0:16, :].reshape(256, 128)
            right = recv[p, pl.ds(u * 16, 16), 16:32, :].reshape(256, 128)
            both = jnp.concatenate([left, right], axis=1)
            out = dot(pack[0 : 3 * UNIT, :], both)
            at = pl.ds(pl.multiple_of(u * UNIT, UNIT), UNIT)
            if p == 0:
                gate = jnp.where(slot_lane, dot(pack[3 * UNIT :, :], left), 0.0)
                scale_col[at, :] = jnp.broadcast_to(jnp.sum(gate, axis=1, keepdims=True), (UNIT, 128))
            for side in range(2):
                for i in range(3):
                    block = out[i * UNIT : (i + 1) * UNIT, side * 128 : (side + 1) * 128]
                    b = side * 3 + i
                    if p < 2:
                        x_rows[at, first + b * 128 : first + (b + 1) * 128] = block.astype(bf16)
                    else:
                        dy_half[at, b * 128 : (b + 1) * 128] = block.astype(bf16)
                        scaled[at, first + b * 128 : first + (b + 1) * 128] = (
                            scale_col[at, :] * block
                        ).astype(bf16)

    unpack(0)
    wait_all(win, w_recv.at[0])

    def project(h):
        @pl.loop(0, 3)
        def _(n):
            at = pl.ds(pl.multiple_of(n * 256, 256), 256)
            out = dot(x_rows[:, h * HALF : (h + 1) * HALF], win[h * HALF : (h + 1) * HALF, at])
            gate_up[:, at] = out if h == 0 else gate_up[:, at] + out

    project(0)
    unpack(1)
    project(1)

    @pl.loop(0, 8)
    def _(u):
        at = pl.ds(pl.multiple_of(u * UNIT, UNIT), UNIT)
        g, up = gate_up[at, :FFN], gate_up[at, FFN:]
        sigma = 1.0 / (1.0 + jnp.exp(-g))
        silu = g * sigma
        hidden[at, :] = (silu * up).astype(bf16)
        gate_up[at, :FFN] = up * sigma * (1.0 + g * (1.0 - sigma))
        gate_up[at, FFN:] = silu

    wait_all(wout, w_recv.at[1])

    def gate_sums(h):
        @pl.loop(0, 4)
        def _(q):
            at = pl.ds(pl.multiple_of(q * 160, 160), 160)
            total = jnp.zeros((160, 128), f32)
            for r in range(2):
                out = dot(hidden[at, :], wout[2 * h + r])
                for b in range(3):
                    c = r * 3 + b
                    total = total + out[:, b * 128 : (b + 1) * 128] * dy_half[
                        at, c * 128 : (c + 1) * 128
                    ].astype(f32)
            gg[at, :] = total if h == 0 else gg[at, :] + total

    def out_part(r):
        part_out[r] = dot(hidden[...], scaled[:, r * FFN : (r + 1) * FFN], (0, 0)).astype(bf16)

        @pl.when(rep != r)
        def _():
            slot = (rep - r + REPS - 1) % REPS
            pltpu.make_async_remote_copy(
                part_out.at[r], got_out.at[slot], out_send, out_recv.at[slot],
                device_id=(r, me), device_id_type=by_mesh,
            ).start()

    unpack(2)
    dh[...] = dot(scaled[:, 0:FFN], wout[0], (1, 1)) + dot(scaled[:, FFN:HALF], wout[1], (1, 1))
    out_part(0)
    out_part(1)
    gate_sums(0)

    unpack(3)
    for q in range(4):
        at = pl.ds(q * 160, 160)
        d = (
            dh[at, :]
            + dot(scaled[at, HALF : HALF + FFN], wout[2], (1, 1))
            + dot(scaled[at, HALF + FFN :], wout[3], (1, 1))
        )
        dgu[at, :FFN] = (d * gate_up[at, :FFN]).astype(bf16)
        dgu[at, FFN:] = (d * gate_up[at, FFN:]).astype(bf16)

    def back(h):
        @pl.loop(0, 3)
        def _(n):
            at = pl.ds(pl.multiple_of(n * 256, 256), 256)
            from_in = pl.ds(pl.multiple_of(h * HALF + n * 256, 256), 256)
            row_grad[:, at] = dot(dgu[...], win[from_in, :], (1, 1)).astype(bf16)

        @pl.loop(0, 8)
        def _(u):
            at = pl.ds(pl.multiple_of(u * UNIT, UNIT), UNIT)
            sides = []
            for side in range(2):
                parts = [row_grad[at, (side * 3 + i) * 128 : (side * 3 + i + 1) * 128] for i in range(3)]
                if h == 1:
                    gates_back = jnp.sum(gg[at, :], axis=1, keepdims=True)
                    here = jnp.where(slot_lane, gates_back, 0.0) if side else jnp.zeros((UNIT, 128), f32)
                    parts.append(here.astype(bf16))
                sides.append(jnp.concatenate(parts, axis=0))
            both = jnp.concatenate(sides, axis=1)
            out = dot(pack[0 : both.shape[0], :], both, (0, 0))
            back_send[h, pl.ds(u * 16, 16), 0:16, :] = out[:, :128].reshape(16, 16, 128).astype(bf16)
            back_send[h, pl.ds(u * 16, 16), 16:32, :] = out[:, 128:].reshape(16, 16, 128).astype(bf16)

        send_back(h)

    back(0)

    @pl.loop(1, REPS + 1)
    def _(d):
        r = (rep + d) % REPS
        at = pl.ds(pl.multiple_of(r * FFN, FFN), FFN)
        part_in[r] = dot(x_rows[:, at], dgu[...], (0, 0)).astype(bf16)

        @pl.when(d < REPS)
        def _():
            slot = (REPS - 1 + rep - r + REPS) % REPS
            pltpu.make_async_remote_copy(
                part_in.at[r], got_in.at[slot], in_send, in_recv.at[slot],
                device_id=(r, me), device_id_type=by_mesh,
            ).start()

    out_part(2)
    out_part(3)
    gate_sums(1)
    back(1)

    def combine(h):
        wait_all(back_recv.at[h], back_recv_sem.at[h])
        for side in range(2):
            total = dot(
                pick[...], back_recv[h, :, side * 16 : (side + 1) * 16, :].reshape(PEERS * 16, 128), (0, 0)
            )
            for i in range(3):
                b = h * 6 + side * 3 + i
                token_grad_ref[:, b * 128 : (b + 1) * 128] = total[i * TOK : (i + 1) * TOK, :].astype(bf16)

    combine(0)

    for s in range(REPS - 1):
        wait_all(got_out.at[s], out_recv.at[s])
    new_out_ref[...] = (
        decay * mom_out_ref[...].astype(f32)
        + part_out[rep].astype(f32)
        + sum(got_out[s].astype(f32) for s in range(REPS - 1))
    ).astype(bf16)
    for s in range(REPS - 1):
        wait_all(got_in.at[s], in_recv.at[s])
    new_in_ref[...] = (
        decay * mom_in_ref[...].astype(f32)
        + part_in[rep].astype(f32)
        + sum(got_in[s].astype(f32) for s in range(REPS - 1))
    ).astype(bf16)

    combine(1)
    last = back_recv[1, :, 16:32, :].astype(f32)
    got_gates = jnp.sum(jnp.where(iota((PEERS, 16, 128), 1) == 15, last, 0.0), axis=1)
    sums = [jnp.zeros((1, TOK), f32) for _ in range(TOP)]
    for s in range(CAP):
        value = jnp.sum(jnp.where(lane == s, got_gates, 0.0), axis=1, keepdims=True)
        for k in range(TOP):
            hit = own_key + s == keys[k]
            sums[k] = sums[k] + jnp.sum(jnp.where(hit, value, 0.0), axis=0, keepdims=True)
    gate_grad_ref[...] = jnp.concatenate(sums, axis=0).astype(bf16)

    for p in range(4):
        wait_all(send.at[p, pl.ds(1, PEERS - 1)], send_sem.at[p])
    for h in range(2):
        wait_all(back_send.at[h, pl.ds(1, PEERS - 1)], back_send_sem.at[h])
    wait_all(win.at[pl.ds(0, (REPS - 1) * FFN)], w_send.at[0])
    wait_all(wout.at[pl.ds(0, REPS - 1)], w_send.at[1])
    wait_all(part_in.at[pl.ds(0, REPS - 1)], in_send)
    wait_all(part_out.at[pl.ds(0, REPS - 1)], out_send)


def per_device(tokens, routes, gates, output_grad, w_in, w_out, momentum_in, momentum_out):
    vmem = pl.BlockSpec(memory_space=pltpu.VMEM)
    dma = pltpu.SemaphoreType.DMA
    scratch = [
        pltpu.VMEM((PEERS * 16, 3 * TOK), bf16),
        pltpu.VMEM((4 * UNIT, 256), bf16),
        pltpu.VMEM((PEERS, 128), f32),
        pltpu.VMEM((4, PEERS, 32, 128), bf16),
        pltpu.VMEM((4, PEERS, 32, 128), bf16),
        pltpu.VMEM((2, PEERS, 32, 128), bf16),
        pltpu.VMEM((2, PEERS, 32, 128), bf16),
        pltpu.VMEM((ROWS, WIDTH), bf16),
        pltpu.VMEM((ROWS, WIDTH), bf16),
        pltpu.VMEM((ROWS, HALF), bf16),
        pltpu.VMEM((ROWS, 128), f32),
        pltpu.VMEM((WIDTH, 2 * FFN), bf16),
        pltpu.VMEM((REPS, FFN, FFN), bf16),
        pltpu.VMEM((ROWS, 2 * FFN), f32),
        pltpu.VMEM((ROWS, FFN), bf16),
        pltpu.VMEM((ROWS, FFN), f32),
        pltpu.VMEM((ROWS, 2 * FFN), bf16),
        pltpu.VMEM((ROWS, HALF), bf16),
        pltpu.VMEM((ROWS, 128), f32),
        pltpu.VMEM((REPS, FFN, 2 * FFN), bf16),
        pltpu.VMEM((REPS, FFN, FFN), bf16),
        pltpu.VMEM((REPS - 1, FFN, 2 * FFN), bf16),
        pltpu.VMEM((REPS - 1, FFN, FFN), bf16),
        dma((4,)), dma((4,)), dma((2,)), dma((2,)), dma((2,)), dma((2,)),
        dma, dma((REPS - 1,)), dma, dma((REPS - 1,)),
    ]
    token_grad, gate_grad, new_in, new_out = pl.pallas_call(
        kernel,
        out_shape=(
            jax.ShapeDtypeStruct((TOK, WIDTH), bf16),
            jax.ShapeDtypeStruct((TOP, TOK), bf16),
            jax.ShapeDtypeStruct((FFN, 2 * FFN), bf16),
            jax.ShapeDtypeStruct((FFN, FFN), bf16),
        ),
        in_specs=[vmem] * 8,
        out_specs=(vmem,) * 4,
        scratch_shapes=scratch,
        compiler_params=pltpu.CompilerParams(
            collective_id=0, has_side_effects=True, vmem_limit_bytes=56 * 2**20
        ),
    )(tokens, routes.T, gates.T, output_grad, w_in[0], w_out[0], momentum_in[0], momentum_out[0])
    return token_grad, gate_grad.T, new_in[None], new_out[None]


def solution(mesh):
    rows, w_in, w_out = P(("rep", "expert"), None), P("expert", "rep", None), P("expert", None, "rep")
    return jax.shard_map(
        per_device,
        mesh=mesh,
        in_specs=(rows, rows, rows, rows, w_in, w_out, w_in, w_out),
        out_specs=(rows, rows, w_in, w_out),
        check_vma=False,
    )
```

time: 367 us -> 181 us (0.49)
  waiting for transfers between devices: 203 us -> 0 us
  Pallas kernels: 0 us -> 176 us
  local copies, waits for them, and re-layouts: 57.7 us -> 4.24 us
  starting transfers between devices: 52.4 us -> 0 us
  matrix products: 23 us -> 0 us
  between operations: 14.1 us -> 0.66 us
  other arithmetic: 13.1 us -> 0 us
    all_to_all x4 -> x0, waiting for transfers between devices: 202 us -> none  [the longest x1 72.4 us: in_one_piece(): lax.all_to_all(both, axis, split_axis=split_dim, concat_axis=concat_dim,...]
    pallas_call x0 -> x1, Pallas kernels: none -> 176 us  [per_device(): pl.pallas_call(kernel, out_shape=(jax.ShapeDtypeStruct((TOK, WIDTH), bf16...]
    all_to_all x4 -> x0, starting transfers between devices: 52.3 us -> none  [the longest x1 19 us: per_device(): lax.all_to_all(sent_grads, 'expert', split_axis=0, concat_axis=0, tiled=T...]
    dot_general x6 -> x0, matrix products: 23 us -> none  [the longest x1 5.75 us: forward_pass(): both = jnp.dot(x_rows, weight_in, preferred_element_type=jnp.float32)]
    gather x4 -> x0, local copies, waits for them, and re-layouts: 12.4 us -> none  [the longest x1 3.67 us: per_device(): jnp.concatenate([tokens, zero_row], axis=0)[source_row]]
    convert_element_type x5 -> x0, local copies, waits for them, and re-layouts: 9.79 us -> none  [the longest x1 4.59 us: per_device(): dy_rows.astype(jnp.float32)]
    reshape x8 -> x0, local copies, waits for them, and re-layouts: 9.11 us -> none  [the longest x2 3.39 us: per_device(): back_rows.reshape(slot_count, width)[target]]
    another operation x6 -> x0, local copies, waits for them, and re-layouts: 7.1 us -> none  [the longest x1 4.33 us: local_rows(): return shaped[:, expert].reshape((senders * capacity,) + received.shape[2:])]
  transfers between devices with their start and end apart: 8 -> 0, of which waited for: 4 -> 0; matrix products, arithmetic and copies ran while one was open for 19% -> 0% of each run, Pallas kernels for 0% -> 0%
where the time goes in v1:
time: 181 us
  Pallas kernels  176 us (97%)
  local copies, waits for them, and re-layouts  4.24 us (2%)
    pallas_call x1, Pallas kernels, per_device(): pl.pallas_call(kernel, out_shape=(jax.ShapeDtypeStruct((TOK, WIDTH), bf16...  176 us
    unnamed x10, local copies, waits for them, and re-layouts  4.24 us

profile of v1, /device:TPU:1, one launch (start us, length us, event | category | flops | bytes accessed | tf_op | source)
XLA Modules:
  0.0 180.9 jit_solution(4239320244811821077)
XLA Ops:
  0.6 176.0 %shard_map.111 = (bf16[128,1536]{1,0:T(8,128)(2,1)}, bf16[4,128]{1,0:T(4,128)(2,1)}, bf16[384,768]{1,0:T(8,128)(2,1)}, bf16[384,384]{1,0:T(8,128)(2,1)}) custom-call(bf16[128,1536]{1,0:T(8,128)(2,1)} %tok_ref.1, s32[4,128]{1,0:T(4,128)} %bitcast.15, bf16[4,128]{1,0:T(4,128)(2,1)} %bitcast.16, bf16[128,1536]{1,0:T(8,128)(2,1)} %dy_ref.1, ...), custom_call_target="tpu_custom_call" | custom-call | tf_op jit(solution)/shard_map/pallas_call | solution.py:383
  176.7 0.0 copy-start
  176.7 0.0 copy-start.2
  176.7 1.8 %copy.16 = bf16[128,1536]{1,0:T(8,128)(2,1)} copy(bf16[128,1536]{1,0:T(8,128)(2,1)} %get-tuple-element.16) | data formatting | bytes 786432
  178.5 0.0 copy-done.2
  178.5 0.6 copy.17
  179.1 0.0 copy-done
  179.1 0.0 copy-start.1
  179.1 0.8 copy.18
  179.9 0.3 copy-done.1
  180.2 0.7 copy.19
Async XLA Ops:
  176.7 2.4 %copy-start = (bf16[384,768]{1,0:T(8,128)(2,1)S(1)}, bf16[384,768]{1,0:T(8,128)(2,1)}, u32[]{:S(2)}) copy-start(bf16[384,768]{1,0:T(8,128)(2,1)} %get-tuple-element.10) | copy-start | bytes 1769476
  176.7 1.8 %copy-start.2 = (bf16[4,128]{1,0:T(4,128)(2,1)S(1)}, bf16[4,128]{1,0:T(4,128)(2,1)}, u32[]{:S(2)}) copy-start(bf16[4,128]{1,0:T(4,128)(2,1)} %get-tuple-element.9) | copy-start | bytes 3076
  179.1 1.1 copy-start.1

commit v2 on v1

--- a/solution.py
+++ b/solution.py
@@ -13,6 +13,8 @@
 PEERS, TOK, WIDTH, HALF, FFN, CAP, TOP, REPS = 128, 128, 1536, 768, 384, 5, 4, 4
 ROWS = PEERS * CAP
 UNIT = 16 * CAP
+GROUPS, MEMBERS = 2, 64
+GROUP = MEMBERS * CAP
 by_mesh = pl.DeviceIdType.MESH
 
 
@@ -25,12 +27,12 @@
 
 
 def kernel(
-    tok_ref, routes_ref, gates_ref, dy_ref, w_in_ref, w_out_ref, mom_in_ref, mom_out_ref,
+    tok_any, routes_ref, gates_ref, dy_any, w_in_ref, w_out_ref, mom_in_any, mom_out_any,
     token_grad_ref, gate_grad_ref, new_in_ref, new_out_ref,
-    pick, pack, gate_rows, send, recv, back_send, back_recv,
-    x_rows, scaled, dy_half, scale_col, win, wout, gate_up, hidden, dh, dgu, row_grad, gg,
+    tok_ref, dy_ref, mom_in_ref, mom_out_ref, pick, pick_t, pack, gate_rows, send, recv, back_send, back_recv,
+    x_rows, x_t, scaled, dy_half, scale_col, win, wout, gate_up, win_t, wout_t, hidden, dh, dgu, row_grad, gg,
     part_in, part_out, got_in, got_out,
-    send_sem, recv_sem, back_send_sem, back_recv_sem, w_send, w_recv, in_send, in_recv, out_send, out_recv,
+    send_sem, recv_sem, back_send_sem, back_recv_sem, w_send, w_recv, in_send, in_recv, out_send, out_recv, layers_in, local,
 ):
     rep = lax.axis_index("rep")
     me = lax.axis_index("expert")
@@ -42,13 +44,29 @@
         return ((z + sign * dz + 8) % 8) * 16 + ((y + sign * dy + 8) % 8) * 2 + (core + dc) % 2
 
     barrier = pltpu.get_barrier_semaphore()
-
-    @pl.loop(1, PEERS)
-    def _(j):
-        pl.semaphore_signal(barrier, inc=1, device_id=(rep, peer(j, 1)), device_id_type=by_mesh)
+    in_layer = me % 16
+
+    def greet(sem, to_rep, to):
+        pl.semaphore_signal(sem, inc=1, device_id=(to_rep, to), device_id_type=by_mesh)
+
+    for d in range(1, 8):
+        greet(barrier, rep, ((z + d) % 8) * 16 + in_layer)
+
+    @pl.loop(1, 16)
+    def _(d):
+        greet(barrier, rep, z * 16 + (in_layer + d) % 16)
 
     for d in range(1, REPS):
-        pl.semaphore_signal(barrier, inc=1, device_id=((rep + d) % REPS, me), device_id_type=by_mesh)
+        greet(barrier, (rep + d) % REPS, me)
+
+    inputs = [
+        pltpu.make_async_copy(a, b, local.at[n])
+        for n, (a, b) in enumerate(
+            [(tok_any, tok_ref), (dy_any, dy_ref), (mom_in_any, mom_in_ref), (mom_out_any, mom_out_ref)]
+        )
+    ]
+    for copy in inputs:
+        copy.start()
 
     expert_of = iota((PEERS, TOK), 0)
     before = (iota((TOK, TOK), 0) < iota((TOK, TOK), 1)).astype(f32).astype(bf16)
@@ -117,30 +135,46 @@
             send[p, pl.ds(q * 16, 16), 16:32, :] = out[:, 128:].reshape(16, 16, 128).astype(bf16)
 
     def send_pass(p):
-        pltpu.make_async_copy(send.at[p, 0], recv.at[p, 0], recv_sem.at[p]).start()
-
-        @pl.loop(1, PEERS)
-        def _(j):
-            pltpu.make_async_remote_copy(
-                send.at[p, j], recv.at[p, j], send_sem.at[p], recv_sem.at[p],
-                device_id=(rep, peer(j, 1)), device_id_type=by_mesh,
-            ).start()
-
-    def send_back(h):
-        pltpu.make_async_copy(back_send.at[h, 0], back_recv.at[h, 0], back_recv_sem.at[h]).start()
-
-        @pl.loop(1, PEERS)
-        def _(j):
+        for g in range(GROUPS):
+            arrived = recv_sem.at[3 + g if p == 3 else p]
+            if g == 0:
+                pltpu.make_async_copy(send.at[p, 0], recv.at[p, 0], arrived).start()
+
+            @pl.loop(max(1, g * MEMBERS), (g + 1) * MEMBERS)
+            def _(j):
+                pltpu.make_async_remote_copy(
+                    send.at[p, j], recv.at[p, j], send_sem.at[p], arrived,
+                    device_id=(rep, peer(j, 1)), device_id_type=by_mesh,
+                ).start()
+
+    def send_back(h, g):
+        def one(j):
             pltpu.make_async_remote_copy(
                 back_send.at[h, j], back_recv.at[h, j], back_send_sem.at[h], back_recv_sem.at[h],
                 device_id=(rep, peer(j, -1)), device_id_type=by_mesh,
             ).start()
 
+        @pl.when(g > 0)
+        def _():
+            one(g * MEMBERS)
+
+        @pl.when(g == 0)
+        def _():
+            pltpu.make_async_copy(back_send.at[h, 0], back_recv.at[h, 0], back_recv_sem.at[h]).start()
+
+        @pl.loop(1, MEMBERS)
+        def _(i):
+            one(g * MEMBERS + i)
+
     def wait_all(ref, sem):
         pltpu.make_async_copy(ref, ref, sem).wait()
 
+    pl.semaphore_wait(barrier, 7 + 15 + REPS - 1)
+    for d in range(1, 8):
+        greet(layers_in, rep, ((z + d) % 8) * 16 + in_layer)
+    inputs[0].wait()
     gather(0)
-    pl.semaphore_wait(barrier, PEERS - 1 + REPS - 1)
+    pl.semaphore_wait(layers_in, 7)
     send_pass(0)
 
     mine = pl.ds(pl.multiple_of(rep * FFN, FFN), FFN)
@@ -158,16 +192,17 @@
             w_out_ref, wout.at[rep], w_send.at[1], w_recv.at[1],
             device_id=((rep + d) % REPS, me), device_id_type=by_mesh,
         ).start()
+    inputs[1].wait()
     for p in range(1, 4):
         gather(p)
         send_pass(p)
 
-    def unpack(p):
-        wait_all(recv.at[p], recv_sem.at[p])
+    def unpack(p, start=0, units=8):
         first = (p % 2) * HALF
 
-        @pl.loop(0, 8)
-        def _(u):
+        @pl.loop(0, units)
+        def _(step):
+            u = start + step
             left = recv[p, pl.ds(u * 16, 16), 0:16, :].reshape(256, 128)
             right = recv[p, pl.ds(u * 16, 16), 16:32, :].reshape(256, 128)
             both = jnp.concatenate([left, right], axis=1)
@@ -188,6 +223,7 @@
                             scale_col[at, :] * block
                         ).astype(bf16)
 
+    wait_all(recv.at[0], recv_sem.at[0])
     unpack(0)
     wait_all(win, w_recv.at[0])
 
@@ -199,8 +235,17 @@
             gate_up[:, at] = out if h == 0 else gate_up[:, at] + out
 
     project(0)
+    wait_all(recv.at[1], recv_sem.at[1])
     unpack(1)
     project(1)
+
+    @pl.loop(0, REPS)
+    def _(r):
+        at = pl.ds(pl.multiple_of(r * FFN, FFN), FFN)
+        x_t[at, :] = x_rows[:, at].T
+        win_t[:, at] = win[at, :].T
+        block = pl.ds(pl.multiple_of(r * 512, 512), 512)
+        pick_t[:, block] = pick[block, :].T
 
     @pl.loop(0, 8)
     def _(u):
@@ -214,19 +259,21 @@
 
     wait_all(wout, w_recv.at[1])
 
-    def gate_sums(h):
-        @pl.loop(0, 4)
-        def _(q):
-            at = pl.ds(pl.multiple_of(q * 160, 160), 160)
-            total = jnp.zeros((160, 128), f32)
-            for r in range(2):
-                out = dot(hidden[at, :], wout[2 * h + r])
-                for b in range(3):
-                    c = r * 3 + b
-                    total = total + out[:, b * 128 : (b + 1) * 128] * dy_half[
-                        at, c * 128 : (c + 1) * 128
-                    ].astype(f32)
-            gg[at, :] = total if h == 0 else gg[at, :] + total
+    @pl.loop(0, REPS)
+    def _(r):
+        wout_t[r] = wout[r].T
+
+    def gate_sums(h, g):
+        at = pl.ds(pl.multiple_of(g * GROUP, GROUP), GROUP)
+        total = jnp.zeros((GROUP, 128), f32) if h == 0 else gg[at, :]
+        for r in range(2):
+            out = dot(hidden[at, :], wout[2 * h + r])
+            for b in range(3):
+                c = r * 3 + b
+                total = total + out[:, b * 128 : (b + 1) * 128] * dy_half[
+                    at, c * 128 : (c + 1) * 128
+                ].astype(f32)
+        gg[at, :] = total
 
     def out_part(r):
         part_out[r] = dot(hidden[...], scaled[:, r * FFN : (r + 1) * FFN], (0, 0)).astype(bf16)
@@ -239,32 +286,20 @@
                 device_id=(r, me), device_id_type=by_mesh,
             ).start()
 
+    wait_all(recv.at[2], recv_sem.at[2])
     unpack(2)
-    dh[...] = dot(scaled[:, 0:FFN], wout[0], (1, 1)) + dot(scaled[:, FFN:HALF], wout[1], (1, 1))
+    dh[...] = dot(scaled[:, 0:FFN], wout_t[0]) + dot(scaled[:, FFN:HALF], wout_t[1])
     out_part(0)
     out_part(1)
-    gate_sums(0)
-
-    unpack(3)
-    for q in range(4):
-        at = pl.ds(q * 160, 160)
-        d = (
-            dh[at, :]
-            + dot(scaled[at, HALF : HALF + FFN], wout[2], (1, 1))
-            + dot(scaled[at, HALF + FFN :], wout[3], (1, 1))
-        )
-        dgu[at, :FFN] = (d * gate_up[at, :FFN]).astype(bf16)
-        dgu[at, FFN:] = (d * gate_up[at, FFN:]).astype(bf16)
-
-    def back(h):
-        @pl.loop(0, 3)
-        def _(n):
-            at = pl.ds(pl.multiple_of(n * 256, 256), 256)
-            from_in = pl.ds(pl.multiple_of(h * HALF + n * 256, 256), 256)
-            row_grad[:, at] = dot(dgu[...], win[from_in, :], (1, 1)).astype(bf16)
-
-        @pl.loop(0, 8)
-        def _(u):
+    pl.loop(0, GROUPS)(lambda g: gate_sums(0, g))
+
+    def row_grads(h, g):
+        rows = pl.ds(pl.multiple_of(g * GROUP, GROUP), GROUP)
+        row_grad[rows, :] = dot(dgu[rows, :], win_t[:, h * HALF : (h + 1) * HALF]).astype(bf16)
+
+        @pl.loop(0, GROUP // UNIT)
+        def _(step):
+            u = g * (GROUP // UNIT) + step
             at = pl.ds(pl.multiple_of(u * UNIT, UNIT), UNIT)
             sides = []
             for side in range(2):
@@ -279,40 +314,70 @@
             back_send[h, pl.ds(u * 16, 16), 0:16, :] = out[:, :128].reshape(16, 16, 128).astype(bf16)
             back_send[h, pl.ds(u * 16, 16), 16:32, :] = out[:, 128:].reshape(16, 16, 128).astype(bf16)
 
-        send_back(h)
-
-    back(0)
-
-    @pl.loop(1, REPS + 1)
+    def arrival(g):
+        wait_all(recv.at[3, pl.ds(g * MEMBERS, MEMBERS)], recv_sem.at[3 + g])
+
+    def first_half(g):
+        unpack(3, g * (GROUP // UNIT), GROUP // UNIT)
+        at = pl.ds(pl.multiple_of(g * GROUP, GROUP), GROUP)
+        d = (
+            dh[at, :]
+            + dot(scaled[at, HALF : HALF + FFN], wout_t[2])
+            + dot(scaled[at, HALF + FFN :], wout_t[3])
+        )
+        dgu[at, :FFN] = (d * gate_up[at, :FFN]).astype(bf16)
+        dgu[at, FFN:] = (d * gate_up[at, FFN:]).astype(bf16)
+        row_grads(0, g)
+
+    def second_half(g):
+        gate_sums(1, g)
+        row_grads(1, g)
+
+    @pl.loop(0, GROUPS)
+    def _(g):
+        arrival(g)
+
+        @pl.when(g == GROUPS - 1)
+        def _():
+            pl.loop(0, GROUPS - 1)(lambda k: send_back(0, k))
+
+        first_half(g)
+
+        @pl.when(g < GROUPS - 1)
+        def _():
+            second_half(g)
+
+    send_back(0, GROUPS - 1)
+
+    @pl.loop(1, REPS)
     def _(d):
         r = (rep + d) % REPS
-        at = pl.ds(pl.multiple_of(r * FFN, FFN), FFN)
-        part_in[r] = dot(x_rows[:, at], dgu[...], (0, 0)).astype(bf16)
-
-        @pl.when(d < REPS)
-        def _():
-            slot = (REPS - 1 + rep - r + REPS) % REPS
-            pltpu.make_async_remote_copy(
-                part_in.at[r], got_in.at[slot], in_send, in_recv.at[slot],
-                device_id=(r, me), device_id_type=by_mesh,
-            ).start()
-
+        part_in[r] = dot(x_t[pl.ds(pl.multiple_of(r * FFN, FFN), FFN), :], dgu[...]).astype(bf16)
+        slot = REPS - 1 - d
+        pltpu.make_async_remote_copy(
+            part_in.at[r], got_in.at[slot], in_send, in_recv.at[slot],
+            device_id=(r, me), device_id_type=by_mesh,
+        ).start()
+
+    second_half(GROUPS - 1)
+    pl.loop(0, GROUPS)(lambda g: send_back(1, g))
     out_part(2)
     out_part(3)
-    gate_sums(1)
-    back(1)
+    part_in[rep] = dot(x_t[mine, :], dgu[...]).astype(bf16)
 
     def combine(h):
         wait_all(back_recv.at[h], back_recv_sem.at[h])
         for side in range(2):
             total = dot(
-                pick[...], back_recv[h, :, side * 16 : (side + 1) * 16, :].reshape(PEERS * 16, 128), (0, 0)
+                pick_t[...], back_recv[h, :, side * 16 : (side + 1) * 16, :].reshape(PEERS * 16, 128)
             )
             for i in range(3):
                 b = h * 6 + side * 3 + i
                 token_grad_ref[:, b * 128 : (b + 1) * 128] = total[i * TOK : (i + 1) * TOK, :].astype(bf16)
 
     combine(0)
+    inputs[2].wait()
+    inputs[3].wait()
 
     for s in range(REPS - 1):
         wait_all(got_out.at[s], out_recv.at[s])
@@ -353,8 +418,14 @@
 def per_device(tokens, routes, gates, output_grad, w_in, w_out, momentum_in, momentum_out):
     vmem = pl.BlockSpec(memory_space=pltpu.VMEM)
     dma = pltpu.SemaphoreType.DMA
+    any_space = pl.BlockSpec(memory_space=pl.ANY)
     scratch = [
+        pltpu.VMEM((TOK, WIDTH), bf16),
+        pltpu.VMEM((TOK, WIDTH), bf16),
+        pltpu.VMEM((FFN, 2 * FFN), bf16),
+        pltpu.VMEM((FFN, FFN), bf16),
         pltpu.VMEM((PEERS * 16, 3 * TOK), bf16),
+        pltpu.VMEM((3 * TOK, PEERS * 16), bf16),
         pltpu.VMEM((4 * UNIT, 256), bf16),
         pltpu.VMEM((PEERS, 128), f32),
         pltpu.VMEM((4, PEERS, 32, 128), bf16),
@@ -362,12 +433,15 @@
         pltpu.VMEM((2, PEERS, 32, 128), bf16),
         pltpu.VMEM((2, PEERS, 32, 128), bf16),
         pltpu.VMEM((ROWS, WIDTH), bf16),
+        pltpu.VMEM((WIDTH, ROWS), bf16),
         pltpu.VMEM((ROWS, WIDTH), bf16),
         pltpu.VMEM((ROWS, HALF), bf16),
         pltpu.VMEM((ROWS, 128), f32),
         pltpu.VMEM((WIDTH, 2 * FFN), bf16),
         pltpu.VMEM((REPS, FFN, FFN), bf16),
         pltpu.VMEM((ROWS, 2 * FFN), f32),
+        pltpu.VMEM((2 * FFN, WIDTH), bf16),
+        pltpu.VMEM((REPS, FFN, FFN), bf16),
         pltpu.VMEM((ROWS, FFN), bf16),
         pltpu.VMEM((ROWS, FFN), f32),
         pltpu.VMEM((ROWS, 2 * FFN), bf16),
@@ -377,18 +451,18 @@
         pltpu.VMEM((REPS, FFN, FFN), bf16),
         pltpu.VMEM((REPS - 1, FFN, 2 * FFN), bf16),
         pltpu.VMEM((REPS - 1, FFN, FFN), bf16),
-        dma((4,)), dma((4,)), dma((2,)), dma((2,)), dma((2,)), dma((2,)),
-        dma, dma((REPS - 1,)), dma, dma((REPS - 1,)),
+        dma((4,)), dma((3 + GROUPS,)), dma((2,)), dma((2,)), dma((2,)), dma((2,)),
+        dma, dma((REPS - 1,)), dma, dma((REPS - 1,)), pltpu.SemaphoreType.REGULAR, dma((4,)),
     ]
     token_grad, gate_grad, new_in, new_out = pl.pallas_call(
         kernel,
         out_shape=(
-            jax.ShapeDtypeStruct((TOK, WIDTH), bf16),
-            jax.ShapeDtypeStruct((TOP, TOK), bf16),
-            jax.ShapeDtypeStruct((FFN, 2 * FFN), bf16),
-            jax.ShapeDtypeStruct((FFN, FFN), bf16),
+            pltpu.VMEM((TOK, WIDTH), bf16),
+            pltpu.VMEM((TOP, TOK), bf16),
+            pltpu.VMEM((FFN, 2 * FFN), bf16),
+            pltpu.VMEM((FFN, FFN), bf16),
         ),
-        in_specs=[vmem] * 8,
+        in_specs=[any_space, vmem, vmem] + [any_space] * 5,
         out_specs=(vmem,) * 4,
         scratch_shapes=scratch,
         compiler_params=pltpu.CompilerParams(

time: 181 us -> 173 us (0.956); the launches traced: 181 us -> 171 us
  Pallas kernels: 176 us -> 167 us
    pallas_call x1, Pallas kernels: 176 us -> 167 us  [per_device(): pl.pallas_call(kernel, out_shape=(pltpu.VMEM((TOK, WIDTH), bf16), pltpu.V...]
    unnamed x10 -> x4, local copies, waits for them, and re-layouts: 4.24 us -> 2.84 us
where the time goes in v2:
time: 173 us; the launch traced here: 171 us
  Pallas kernels  167 us (97%)
  local copies, waits for them, and re-layouts  2.84 us (2%)
    pallas_call x1, Pallas kernels, per_device(): pl.pallas_call(kernel, out_shape=(pltpu.VMEM((TOK, WIDTH), bf16), pltpu.V...  167 us

profile of v2, /device:TPU:1, one launch (start us, length us, event | category | flops | bytes accessed | tf_op | source)
XLA Modules:
  0.0 170.9 jit_solution(3570907298477485100)
XLA Ops:
  0.6 167.4 %shard_map.111 = (bf16[128,1536]{1,0:T(8,128)(2,1)S(1)}, bf16[4,128]{1,0:T(4,128)(2,1)S(1)}, bf16[384,768]{1,0:T(8,128)(2,1)S(1)}, bf16[384,384]{1,0:T(8,128)(2,1)S(1)}) custom-call(bf16[128,1536]{1,0:T(8,128)(2,1)} %tok_any.1, s32[4,128]{1,0:T(4,128)} %bitcast.16, bf16[4,128]{1,0:T(4,128)(2,1)} %bitcast.17, bf16[128,1536]{1,0:T(8,128)(2,1)} %dy_any.1, ...), custom_call_target="tpu_custom_call" | custom-call | tf_op jit(solution)/shard_map/pallas_call | solution.py:457
  168.1 0.7 copy.16
  168.8 0.6 copy.17
  169.4 0.7 copy.19
  170.1 0.8 copy.18

commit v3 on v2

--- a/solution.py
+++ b/solution.py
@@ -40,7 +40,7 @@
 
     def peer(j, sign):
         m = j // 2
-        dz, dy, dc = m % 8, (m // 8 + m) % 8, j % 2
+        dz, dy, dc = (m % 2) * 4 + (m % 8) // 2, (m // 8 + m) % 8, j % 2
         return ((z + sign * dz + 8) % 8) * 16 + ((y + sign * dy + 8) % 8) * 2 + (core + dc) % 2
 
     barrier = pltpu.get_barrier_semaphore()
@@ -84,7 +84,7 @@
 
     def key_of(j):
         m = j >> 1
-        ez = (z + (m & 7)) & 7
+        ez = (z + ((m & 1) * 4 + ((m & 7) >> 1))) & 7
         ey = (y + (((m >> 3) + m) & 7)) & 7
         return (ez * 16 + ey * 2 + ((core + (j & 1)) & 1)) * 8
 

time: 173 us -> 168 us (0.971)
  Pallas kernels: 167 us -> 163 us
    pallas_call x1, Pallas kernels: 167 us -> 163 us  [per_device(): pl.pallas_call(kernel, out_shape=(pltpu.VMEM((TOK, WIDTH), bf16), pltpu.V...]
where the time goes in v3:
time: 168 us; the launch traced here: 166 us
  Pallas kernels  163 us (97%)
  local copies, waits for them, and re-layouts  2.84 us (2%)
    pallas_call x1, Pallas kernels, per_device(): pl.pallas_call(kernel, out_shape=(pltpu.VMEM((TOK, WIDTH), bf16), pltpu.V...  163 us

profile of v3, /device:TPU:1, one launch (start us, length us, event | category | flops | bytes accessed | tf_op | source)
XLA Modules:
  0.0 166.3 jit_solution(598601035622416651)
XLA Ops:
  0.6 162.8 %shard_map.111 = (bf16[128,1536]{1,0:T(8,128)(2,1)S(1)}, bf16[4,128]{1,0:T(4,128)(2,1)S(1)}, bf16[384,768]{1,0:T(8,128)(2,1)S(1)}, bf16[384,384]{1,0:T(8,128)(2,1)S(1)}) custom-call(bf16[128,1536]{1,0:T(8,128)(2,1)} %tok_any.1, s32[4,128]{1,0:T(4,128)} %bitcast.16, bf16[4,128]{1,0:T(4,128)(2,1)} %bitcast.17, bf16[128,1536]{1,0:T(8,128)(2,1)} %dy_any.1, ...), custom_call_target="tpu_custom_call" | custom-call | tf_op jit(solution)/shard_map/pallas_call | solution.py:457
  163.4 0.7 copy.16
  164.2 0.6 copy.17
  164.7 0.7 copy.19
  165.4 0.8 copy.18
